TPU v7x, 128 devices: a whole 4x4x4 slice. The times are simulated.
128 devices in a mesh: facade: 8 (over z, core), sensor: 16 (over x, y).
Axes of the slice: x: 4, y: 4, z: 4, core: 2. Of those that a mesh axis runs over, the one named last changes fastest.
Arguments:
- sky: bfloat16 [2305, 512], P(None, 'sensor'), may hold values from 0.19921875 to 5
- daylight: bfloat16 [512, 145, 2305], P(('facade', 'sensor')), may hold values from -0.125 to 0.125
- bsdf: bfloat16 [512, 145, 145], P(('facade', 'sensor')), may hold values from -0.5 to 0.5
- view: bfloat16 [128, 288, 145, 256], P('sensor', 'facade'), may hold values from -0.0390625 to 0.0390625
- visible: int32 [128, 288], P('sensor', 'facade'), may hold values from 0 to 63, as said below
- counts: int32 [128, 8], P('sensor', 'facade'), may hold values from 9 to 36, as said below
Outputs:
- illuminance: float32 [128, 256, 512], P(('sensor', 'facade'))
Inputs may be any that keep to these rules, and one draw needn't show every extreme that they name: `visible`: ids are counted within a facade row; the group with id r belongs to the sensor index r // 4 of that row. Over the used slots of one sensor index's 8 blocks in one facade row, exactly 2 distinct groups of every source sensor index appear. Unused slots also name groups of the row. `counts`: in every facade row, some block of each sensor index uses all 36 slots.
All inputs are finite; a program needn't handle non-finite values.
Results may differ from a plain program's by a relative error of at most 0.0041.
Values may be sent and summed in bfloat16 or wider, within the bound.
A program may use at most 192 MiB of HBM per device.

v0:
```python
import jax
import jax.numpy as jnp
from jax import lax
from jax.sharding import PartitionSpec as P


def on_device(sky, daylight, bsdf, view, visible, counts):
    groups_here, klems, patches = daylight.shape
    flat = daylight.reshape(groups_here * klems, patches)
    daylit = jnp.dot(
        flat, lax.all_gather(sky, "sensor", axis=1, tiled=True), preferred_element_type=jnp.float32
    )
    hours = daylit.shape[1]
    daylit = daylit.astype(jnp.bfloat16).reshape(groups_here, klems, hours)
    exitance = jnp.einsum("gkl,glh->gkh", bsdf, daylit, preferred_element_type=jnp.float32)
    exitance = exitance.astype(jnp.bfloat16)
    blocks_here, slots = visible.shape
    used = jnp.arange(slots, dtype=jnp.int32)[None, :] < counts
    table = lax.all_gather(exitance, "sensor", axis=0, tiled=True)
    chosen = table[visible]
    chosen = jnp.where(used[:, :, None, None], chosen, jnp.zeros((), jnp.bfloat16))
    return lax.psum_scatter(
        jnp.einsum("bjks,bjkh->bsh", view, chosen, preferred_element_type=jnp.float32),
        "facade",
        scatter_dimension=0,
        tiled=True,
    )


def solution(mesh):
    placed = (
        P(None, "sensor"),
        P(("facade", "sensor"), None, None),
        P(("facade", "sensor"), None, None),
        P("sensor", "facade", None, None),
        P("sensor", "facade"),
        P("sensor", "facade"),
    )
    return jax.shard_map(
        on_device,
        mesh=mesh,
        in_specs=placed,
        out_specs=P(("sensor", "facade"), None, None),
        check_vma=False,
    )
```

profile of v0, /device:TPU:1, one launch (start us, length us, event | category | flops | bytes accessed | tf_op | source)
XLA Modules:
  0.0 236.6 jit_solution(16541552632468859686)
XLA Ops:
  6.5 0.0 copy-start
  6.5 0.0 all-gather.3.cloned.1.call-start
  6.5 0.7 all-gather.3.cloned.1.call-update
  7.3 0.0 all-gather.5.cloned.1.call-start
  7.3 2.1 copy.14
  9.4 2.9 %reshape.28 = bf16[580,2305]{1,0:T(8,128)(2,1)} reshape(bf16[4,145,2305]{2,1,0:T(8,128)(2,1)S(1)} %copy.14) | data formatting | bytes 5347600 | tf_op jit(solution)/shard_map/reshape | solution.py:9
  12.4 45.6 %all-gather.3.cloned.1.call-done = bf16[2305,512]{0,1:T(8,128)(2,1)} async-done(((bf16[2305,32]{0,1:T(8,128)(2,1)}), bf16[2305,512]{0,1:T(8,128)(2,1)}) %all-gather.3.cloned.1.call-update) | async-done | bytes 2360336 | tf_op jit(solution)/shard_map/all_gather | solution.py:11
  58.0 4.3 %convolution_convert_fusion.1 = bf16[580,512]{1,0:T(8,128)(2,1)S(1)} fusion(bf16[580,2305]{1,0:T(8,128)(2,1)} %reshape.28, bf16[2305,512]{0,1:T(8,128)(2,1)} %all-gather.3.cloned.1.call-done), kind=kOutput, calls=%fused_computation.8 | convolution fusion | flops 1369282560 | bytes 5628040 | tf_op jit(solution)/shard_map/dot_general | solution.py:10
  62.3 0.2 reshape.29
  62.5 0.0 copy-done
  62.5 1.1 fusion.10
  63.6 0.0 all-gather.5.cloned.1.call-update
  63.6 0.0 reduce-scatter.2.cloned.1.call-start
  63.7 0.0 copy-done.2
  63.7 0.1 reshape.32
  63.8 0.0 copy-done.3
  63.8 0.1 iota_compare_fusion
  63.9 77.8 %all-gather.5.cloned.1.call-done = bf16[64,145,512]{2,1,0:T(8,128)(2,1)} async-done(((bf16[4,145,512]{2,1,0:T(8,128)(2,1)}), bf16[64,145,512]{2,1,0:T(8,128)(2,1)}) %all-gather.5.cloned.1.call-update) | async-done | bytes 9502736 | tf_op jit(solution)/shard_map/all_gather | solution.py:19
  141.7 21.3 %gather_fusion = bf16[288,145,512]{2,1,0:T(8,128)(2,1)} fusion(bf16[64,145,512]{2,1,0:T(8,128)(2,1)} %all-gather.5.cloned.1.call-done, s32[1024]{0:T(1024)S(1)} %pad_clamp_fusion), kind=kCustom, calls=%fused_computation | custom fusion | bytes 85525632 | tf_op jit(solution)/shard_map/gather | solution.py:20
  163.0 29.9 %fusion.5 = f32[8,256,512]{1,2,0:T(8,128)} fusion(bf16[8,36,145,256]{3,0,2,1:T(8,128)(2,1)} %param.9, bf16[8,36,145,512]{3,2,1,0:T(8,128)(2,1)} %bitcast.12, pred[8,36]{1,0:T(8,128)(4,1)S(1)} %iota_compare_fusion), kind=kOutput, calls=%fused_computation.6 | convolution fusion | flops 10968514560 | bytes 68337952 | tf_op jit(solution)/shard_map/bjks,bjkh->bsh/dot_general | solution.py:23
  192.9 0.0 reduce-scatter.2.cloned.1.call-update
  192.9 35.1 %reduce-scatter.2.cloned.1.call-done = f32[1,256,512]{1,2,0:T(8,128)} async-done(((f32[8,256,512]{1,2,0:T(8,128)}), f32[1,256,512]{1,2,0:T(8,128)}) %reduce-scatter.2.cloned.1.call-update) | async-done | bytes 524304 | tf_op jit(solution)/shard_map/reduce_scatter | solution.py:22
  228.0 2.0 copy.17
  230.1 0.0 copy-done.1
  (5 shorter events, 0.0 us)
Async XLA Ops:
  6.5 55.9 %copy-start = (bf16[4,145,145]{2,0,1:T(4,128)(2,1)S(1)}, bf16[4,145,145]{2,0,1:T(4,128)(2,1)}, u32[]{:S(2)}) copy-start(bf16[4,145,145]{2,0,1:T(4,128)(2,1)} %param.8) | copy-start | bytes 504604
  6.5 51.4 %all-gather.3.cloned.1.call-start = ((), (), s32[]{:S(2)}) async-start(), calls=%async_computation.1 | async-start | bytes 2646016 | tf_op jit(solution)/shard_map/all_gather | solution.py:11
  7.3 134.4 %all-gather.5.cloned.1.call-start = ((), (), s32[]{:S(2)}) async-start(), calls=%async_computation.2 | async-start | bytes 10584064 | tf_op jit(solution)/shard_map/all_gather | solution.py:19
  12.4 51.3 %copy-start.2 = (s32[8,36]{1,0:T(8,128)S(1)}, s32[8,36]{1,0:T(8,128)}, u32[]{:S(2)}) copy-start(s32[8,36]{1,0:T(8,128)} %param.10) | copy-start | bytes 3460
  12.4 51.4 %copy-start.3 = (s32[8,1]{0,1:T(1,128)S(1)}, s32[8,1]{0,1:T(1,128)}, u32[]{:S(2)}) copy-start(s32[8,1]{0,1:T(1,128)} %param.11) | copy-start | bytes 100
  63.6 164.4 %reduce-scatter.2.cloned.1.call-start = ((), (), s32[]{:S(2)}) async-start(), calls=%async_computation.3 | async-start | bytes 4718592 | tf_op jit(solution)/shard_map/reduce_scatter | solution.py:22
  163.0 67.0 %copy-start.1 = (bf16[4,145,145]{2,0,1:T(4,128)(2,1)S(1)}, bf16[4,145,145]{2,0,1:T(4,128)(2,1)}, u32[]{:S(2)}) copy-start(bf16[4,145,145]{2,0,1:T(4,128)(2,1)} %param.8) | copy-start | bytes 504604
Sparse Core Ops, SparseCore 0:
  9.5 48.3 all-gather.2
  63.8 77.9 all-gather.4
  193.1 34.9 reduce-scatter.1
where the time goes:
time: 239 us; the launch traced here: 237 us
  waiting for transfers between devices  159 us (67%)
  matrix products  35.3 us (15%)
  local copies, waits for them, and re-layouts  28.7 us (12%)
  between operations  13.2 us (6%)
    all_gather x1, waiting for transfers between devices, on_device(): table = lax.all_gather(exitance, 'sensor', axis=0, tiled=True)  77.8 us
    all_gather x1, waiting for transfers between devices, on_device(): lax.all_gather(sky, 'sensor', axis=1, tiled=True)  45.6 us
    reduce_scatter x1, waiting for transfers between devices, on_device(): lax.psum_scatter(jnp.einsum('bjks,bjkh->bsh', view, chosen, preferred_ele...  35.1 us
    dot_general x1, matrix products, on_device(): jnp.einsum('bjks,bjkh->bsh', view, chosen, preferred_element_type=jnp.flo...  29.9 us
    gather x1, local copies, waits for them, and re-layouts, on_device(): chosen = table[visible]  21.3 us
  transfers between devices with their start and end apart: 3, of which 3 were waited for; matrix products, arithmetic and copies ran while one was open for 2% of the time, Pallas kernels for 0%

commit v1 on v0

v1 whole, which is shorter than its diff:
```python
import functools

import jax
import jax.numpy as jnp
from jax import lax
from jax.experimental import pallas as pl
from jax.experimental.pallas import tpu as pltpu
from jax.sharding import PartitionSpec as P

MESH = pl.DeviceIdType.MESH
BF = jnp.bfloat16
F32 = jnp.float32
I32 = jnp.int32

CHUNKS = 4
HC = 128
BUFS = 4


def iota(shape, dim):
    return lax.broadcasted_iota(I32, shape, dim)


def nt(a, b):
    return lax.dot_general(a, b, (((1,), (1,)), ((), ())), preferred_element_type=F32)


def mm(a, b):
    return jnp.dot(a, b, preferred_element_type=F32)


def kernel(sky, day, bsdf, view, vis_v, vis_s, cnt, out,
           skyv, dayv, bsdfv, bexp, vbuf, v2,
           e0, e1, e2, e3, m0, m1, m2, m3,
           s2m, s2r, r2r, trem, selb, selp, qsel, eidx, sels, rss, rsr, own, perm,
           lsem, vsem, k1s, k1r, k2s, k2r, kcs, kcr, ls_s, ls_r,
           p1s, p1r, p2ms, p2mr, p2rs, p2rr, rs_s, rs_r):
    e1buf = [e0, e1, e2, e3]
    r2m = [m0, m1, m2, m3]
    f = lax.axis_index("facade")
    s = lax.axis_index("sensor")
    z, o = f // 2, f % 2
    x, y = s // 4, s % 4
    a = x * (1 - o) + y * o
    b = y * (1 - o) + x * o

    def sid(i, j):
        i, j = i % 4, j % 4
        return (i * 4 + j) * (1 - o) + (j * 4 + i) * o

    def first(d):
        return (f, sid(a + d, b))

    def second(d):
        return (f, sid(a, b + d))

    partner = (z * 2 + (1 - o), s)
    sends = []

    def push(src, dst, ss, rs, dev):
        cp = pltpu.make_async_remote_copy(src_ref=src, dst_ref=dst, send_sem=ss, recv_sem=rs,
                                          device_id=dev, device_id_type=MESH)
        cp.start()
        sends.append(cp)

    def arrived(dst, ss, rs, dev):
        pltpu.make_async_remote_copy(src_ref=dst, dst_ref=dst, send_sem=ss, recv_sem=rs,
                                     device_id=dev, device_id_type=MESH).wait_recv()

    c_sky = pltpu.make_async_copy(sky, skyv.at[s], lsem.at[0])
    c_sky.start()
    c_day = pltpu.make_async_copy(day, dayv, lsem.at[1])
    c_day.start()
    c_bs = pltpu.make_async_copy(bsdf, bsdfv, lsem.at[2])
    c_bs.start()

    def view_copy(j, slot):
        return pltpu.make_async_copy(view.at[j], vbuf.at[slot, pl.ds(0, 145)], vsem.at[slot])

    for q in range(BUFS):
        vbuf[q, 145:160] = jnp.zeros((15, 8, 256), BF)
        view_copy(q, q).start()

    barrier = pltpu.get_barrier_semaphore()
    for d in (1, 2, 3):
        pl.semaphore_signal(barrier, inc=1, device_id=first(d), device_id_type=MESH)
        pl.semaphore_signal(barrier, inc=1, device_id=second(d), device_id_type=MESH)
    for d in range(1, 8):
        pl.semaphore_signal(barrier, inc=1, device_id=((f + d) % 8, s), device_id_type=MESH)
    pl.semaphore_wait(barrier, 13)

    half = pl.ds(pl.multiple_of(16 * o, 16), 16)
    other = pl.ds(pl.multiple_of(16 * (1 - o), 16), 16)
    c_sky.wait()
    for d in (1, 3, 2):
        r = skyv.at[s, half]
        push(r, r, k1s.at[d], k1r.at[d], first(d))
    for d in (1, 2, 3):
        r = skyv.at[s, half]
        push(r, r, k2s.at[d, 0], k2r.at[d, 0], second(d))

    vis = vis_v[...]
    slot_no = iota((8, 36), 1)
    row_no = iota((8, 36), 0)
    lim = jnp.zeros((8, 36), I32)
    for q in range(8):
        lim = jnp.where(row_no == q, cnt[0, q], lim)
    used = slot_no < lim
    src = vis >> 2
    grp = vis & 3
    for q in range(16):
        hit = used & (src == q)
        lo = jnp.min(jnp.where(hit, grp, 3))
        hi = jnp.max(jnp.where(hit, grp, 0))
        sels[2 * q] = lo
        sels[2 * q + 1] = hi
        selb[2 * q:2 * q + 1, :] = jnp.full((1, 128), lo, I32)
        selb[2 * q + 1:2 * q + 2, :] = jnp.full((1, 128), hi, I32)
    for d in (1, 2, 3):
        push(selb, selp.at[4 - d], ls_s.at[d], ls_r.at[4 - d], second(d))

    c_bs.wait()
    w1 = (iota((580, 145), 0) // 4 == iota((580, 145), 1)).astype(F32).astype(BF)
    c1 = nt(w1, bsdfv[...]).astype(BF)
    pr, pc = iota((580, 640), 0), iota((580, 640), 1)
    pk, pg = pr // 4, pr % 4
    hit = (pc < 512) & (pc == pg * 128 + pk) & (pk < 128)
    hit = hit | ((pk >= 128) & (pc - 512 == 17 * pg + pk - 128))
    c2 = mm(c1, hit.astype(F32).astype(BF))
    rr = pc - 512
    gcol = jnp.where(pc < 512, pc // 128,
                     (rr >= 17).astype(I32) + (rr >= 34).astype(I32) + (rr >= 51).astype(I32))
    bexp[...] = jnp.where(pg == gcol, c2, 0.0).astype(BF)

    ur, uc = iota((256, 256), 0), iota((256, 256), 1)
    perm[...] = ((uc % 8 == ur // 32) & (uc // 8 == ur % 32)).astype(F32).astype(BF)

    for d in (1, 3, 2):
        n = sid(a - d, b)
        r = skyv.at[n, half]
        arrived(r, k1s.at[d], k1r.at[d], first(d))
        for dd in (1, 2, 3):
            push(r, r, k2s.at[dd, d], k2r.at[dd, d], second(dd))
        push(r, r, kcs.at[0, d], kcr.at[0, d], partner)
    c_day.wait()

    def permute(lo, hi):
        def body(j, carry):
            slot = j % BUFS
            view_copy(j, slot).wait()
            for t in range(5):
                xin = vbuf[slot, 32 * t:32 * t + 32].reshape(256, 256)
                res = mm(perm[...], xin).astype(BF)
                v2[j, :, 32 * t:32 * t + 32, :] = res.reshape(8, 32, 256)

            @pl.when(j + BUFS < 36)
            def _():
                view_copy(j + BUFS, slot).start()
            return carry
        lax.fori_loop(lo, hi, body, 0)

    permute(0, 8)

    for d in (1, 3, 2):
        for i in range(4):
            r = skyv.at[sid(a - i, b - d), half]
            arrived(r, k2s.at[d, i], k2r.at[d, i], second(d))
            push(r, r, kcs.at[d, i], kcr.at[d, i], partner)
    for d in range(4):
        for i in range(4):
            if d or i:
                r = skyv.at[sid(a - d, b - i), other]
                arrived(r, kcs.at[d, i], kcr.at[d, i], partner)

    def daylit(c):
        lhs = skyv[4 * c:4 * c + 4].reshape(HC, 2305)
        dt = nt(lhs, dayv[...]).astype(BF)
        e = mm(dt, bexp[...]).astype(BF)
        for q in range(5):
            e1buf[c][a, q] = e[:, 128 * q:128 * q + 128]
        r = e1buf[c].at[a]
        for d in (1, 3, 2):
            push(r, r, p1s.at[c, d], p1r.at[c, d], first(d))

    def make_q(d):
        lane, col = iota((128, 256), 0), iota((128, 256), 1)
        for i in range(4):
            acc = jnp.zeros((128, 256), F32)
            for m in range(2):
                row = sid(i, b) * 2 + m
                sel = selp[d, pl.ds(row, 1), :]
                sel = jnp.concatenate([sel, sel], axis=1)
                n = 2 * i + m
                c0 = 17 * n if n < 7 else 128
                hit = (lane - col == 17 * sel - c0) & (col >= c0) & (col < c0 + 17)
                acc = acc + hit.astype(F32)
            qsel[d, 128 * i:128 * i + 128, :] = acc.astype(BF)

    def select(c):
        for d in (1, 3, 2):
            arrived(e1buf[c].at[(a - d) % 4], p1s.at[c, d], p1r.at[c, d], first(d))
        lhs = jnp.concatenate([e1buf[c][i, 4] for i in range(4)], axis=1)
        for d in (2, 1, 3, 0):
            rem = mm(lhs, qsel[d]).astype(BF)
            for i in range(4):
                planes = [e1buf[c][i, g] for g in range(4)]
                for m in range(2):
                    row = sid(i, b) * 2 + m
                    sel = selp[d, pl.ds(row, 1), :]
                    pick = planes[0]
                    for g in range(1, 4):
                        pick = jnp.where(sel == g, planes[g].astype(F32), pick.astype(F32)).astype(BF)
                    if d:
                        s2m[c, d, 2 * i + m] = pick
                    else:
                        r2m[c][b * 8 + 2 * i + m] = pick
            if d:
                s2r[c, d, 0] = rem[:, :128]
                s2r[c, d, 1] = rem[:, 128:]
                push(s2m.at[c, d], r2m[c].at[pl.ds(b * 8, 8)], p2ms.at[c, d], p2mr.at[c, d], second(d))
                push(s2r.at[c, d], r2r.at[c, b], p2rs.at[c, d], p2rr.at[c, d], second(d))
            else:
                r2r[c, b, 0] = rem[:, :128]
                r2r[c, b, 1] = rem[:, 128:]

    def received(c):
        for d in (1, 3, 2):
            j = (b - d) % 4
            arrived(r2m[c].at[pl.ds(j * 8, 8)], p2ms.at[c, d], p2mr.at[c, d], second(d))
            arrived(r2r.at[c, j], p2rs.at[c, d], p2rr.at[c, d], second(d))
        keep = iota((HC, 128), 1) < 17

        def body(fb, carry):
            plane = r2r[c, fb, 0].astype(F32)
            for n in range(7):
                v = plane if n == 0 else pltpu.roll(plane, 128 - 17 * n, 1)
                trem[fb * 8 + n] = jnp.where(keep, v, 0.0).astype(BF)
            trem[fb * 8 + 7] = r2r[c, fb, 1]
            return carry
        lax.fori_loop(0, 4, body, 0)

    def compute(c):
        def block(i):
            bb = (f + 1 + i) % 8
            acc = None
            for j in range(36):
                e = eidx[bb * 36 + j]
                lhs = jnp.concatenate([r2m[c][e], trem[e]], axis=1)[:, :160]
                p = mm(lhs, v2[j, bb])
                acc = p if acc is None else acc + p
            return acc

        def body(i, carry):
            rss[c, i] = block(i).astype(BF)
            rs_copy(c, i).start()
            return carry
        lax.fori_loop(0, 7, body, 0)
        own[c] = block(7)

    def rs_copy(c, i):
        return pltpu.make_async_remote_copy(
            src_ref=rss.at[c, i], dst_ref=rsr.at[c, i], send_sem=rs_s.at[c, i], recv_sem=rs_r.at[c, i],
            device_id=((f + 1 + i) % 8, s), device_id_type=MESH)

    def reduce(c):
        def body(i, carry):
            rs_copy(c, i).wait_recv()
            own[c] += rsr[c, i].astype(F32)
            return carry
        lax.fori_loop(0, 7, body, 0)
        out[0, :, HC * c:HC * c + HC] = own[c].T

    daylit(0)
    daylit(1)
    for c in range(CHUNKS):
        r2m[c][32] = jnp.zeros((HC, 128), BF)
    trem[32] = jnp.zeros((HC, 128), BF)

    def entries(n, carry):
        bb, j = n // 36, n % 36
        v = vis_s[bb, j]
        sx, sy, g = v // 16, (v // 4) % 4, v % 4
        m = jnp.where(g == sels[2 * (v // 4) + 1], 1, 0)
        ia = sx * (1 - o) + sy * o
        fb = sy * (1 - o) + sx * o
        eidx[n] = jnp.where(j < cnt[0, bb], fb * 8 + ia * 2 + m, 32)
        return carry
    lax.fori_loop(0, 288, entries, 0)

    selp[0] = selb[...]
    for d in (1, 2, 3):
        arrived(selp.at[d], ls_s.at[d], ls_r.at[d], second(d))
    for d in range(4):
        make_q(d)
    select(0)
    daylit(2)
    permute(8, 16)
    select(1)
    daylit(3)
    permute(16, 26)
    select(2)
    permute(26, 36)
    select(3)
    for c in range(CHUNKS):
        received(c)
        compute(c)
        if c:
            reduce(c - 1)
    reduce(CHUNKS - 1)
    for cp in sends:
        cp.wait_send()

    def drain(n, carry):
        rs_copy(n // 7, n % 7).wait_send()
        return carry
    lax.fori_loop(0, 7 * CHUNKS, drain, 0)


def on_device(sky, daylight, bsdf, view, visible, counts):
    skyt = sky.T
    day = daylight.transpose(1, 0, 2).reshape(580, 2305)
    bs = bsdf.transpose(1, 0, 2).reshape(580, 145)
    vw = view.transpose(1, 2, 0, 3)
    cnt = counts.T
    V = pltpu.VMEM
    D = pltpu.SemaphoreType.DMA
    anyspec = pl.BlockSpec(memory_space=pl.ANY)
    vm = pl.BlockSpec(memory_space=pltpu.VMEM)
    sm = pl.BlockSpec(memory_space=pltpu.SMEM)
    return pl.pallas_call(
        kernel,
        out_shape=jax.ShapeDtypeStruct((1, 256, 512), F32),
        in_specs=[anyspec, anyspec, anyspec, anyspec, vm, sm, sm],
        out_specs=vm,
        scratch_shapes=[
            V((16, 32, 2305), BF), V((580, 2305), BF), V((580, 145), BF), V((580, 640), BF),
            V((BUFS, 160, 8, 256), BF), V((36, 8, 160, 256), BF),
            *[V((4, 5, HC, 128), BF)] * 4, *[V((33, HC, 128), BF)] * 4,
            V((CHUNKS, 4, 8, HC, 128), BF), V((CHUNKS, 4, 2, HC, 128), BF),
            V((CHUNKS, 4, 2, HC, 128), BF), V((33, HC, 128), BF),
            V((32, 128), I32), V((4, 32, 128), I32), V((4, 512, 256), BF),
            pltpu.SMEM((288,), I32), pltpu.SMEM((32,), I32),
            V((CHUNKS, 7, HC, 256), BF), V((CHUNKS, 7, HC, 256), BF), V((CHUNKS, HC, 256), F32),
            V((256, 256), BF),
            D((3,)), D((BUFS,)), D((4,)), D((4,)), D((4, 4)), D((4, 4)), D((4, 4)), D((4, 4)),
            D((4,)), D((4,)),
            *[D((CHUNKS, 4))] * 6, D((CHUNKS, 7)), D((CHUNKS, 7)),
        ],
        compiler_params=pltpu.CompilerParams(
            collective_id=0, has_side_effects=True, vmem_limit_bytes=60 * 2**20),
    )(skyt, day, bs, vw, visible, visible, cnt)


def solution(mesh):
    placed = (
        P(None, "sensor"),
        P(("facade", "sensor"), None, None),
        P(("facade", "sensor"), None, None),
        P("sensor", "facade", None, None),
        P("sensor", "facade"),
        P("sensor", "facade"),
    )
    return jax.shard_map(
        on_device,
        mesh=mesh,
        in_specs=placed,
        out_specs=P(("sensor", "facade"), None, None),
        check_vma=False,
    )
```

time: 239 us -> 100 us (0.42)
  waiting for transfers between devices: 159 us -> 0 us
  Pallas kernels: 0 us -> 90.7 us
  matrix products: 35.3 us -> 0 us
  local copies, waits for them, and re-layouts: 28.7 us -> 9.2 us
  between operations: 13.2 us -> 0.01 us
    all_gather x2 -> x0, waiting for transfers between devices: 123 us -> none  [the longest x1 77.8 us: on_device(): table = lax.all_gather(exitance, 'sensor', axis=0, tiled=True)]
    pallas_call x0 -> x1, Pallas kernels: none -> 90.7 us  [on_device(): pl.pallas_call(kernel, out_shape=jax.ShapeDtypeStruct((1, 256, 512), F32)...]
    dot_general x3 -> x0, matrix products: 35.3 us -> none  [the longest x1 29.9 us: on_device(): jnp.einsum('bjks,bjkh->bsh', view, chosen, preferred_element_type=jnp.flo...]
    reduce_scatter x1 -> x0, waiting for transfers between devices: 35.1 us -> none  [on_device(): lax.psum_scatter(jnp.einsum('bjks,bjkh->bsh', view, chosen, preferred_ele...]
    gather x1 -> x0, local copies, waits for them, and re-layouts: 21.3 us -> none  [on_device(): chosen = table[visible]]
    reshape x2, local copies, waits for them, and re-layouts: 3.11 us -> 7.33 us  [the longest x1 5.47 us: on_device(): day = daylight.transpose(1, 0, 2).reshape(580, 2305)]
  transfers between devices with their start and end apart: 3 -> 0, of which waited for: 3 -> 0; matrix products, arithmetic and copies ran while one was open for 2% -> 0% of each run, Pallas kernels for 0% -> 0%
where the time goes in v1:
time: 100 us; the launch traced here: 99.9 us
  Pallas kernels  90.7 us (91%)
  local copies, waits for them, and re-layouts  9.2 us (9%)
    pallas_call x1, Pallas kernels, on_device(): pl.pallas_call(kernel, out_shape=jax.ShapeDtypeStruct((1, 256, 512), F32)...  90.7 us
    reshape x1, local copies, waits for them, and re-layouts, on_device(): day = daylight.transpose(1, 0, 2).reshape(580, 2305)  5.47 us

profile of v1, /device:TPU:1, one launch (start us, length us, event | category | flops | bytes accessed | tf_op | source)
XLA Modules:
  0.0 99.9 jit_solution(1973023000803162418)
XLA Ops:
  0.0 1.9 %reshape.7.bsdf = bf16[580,145]{1,0:T(8,128)(2,1)} reshape(bf16[145,4,145]{2,1,0:T(4,128)(2,1)} %bitcast.7) | data formatting | bytes 336400 | tf_op jit(solution)/shard_map/reshape | solution.py:322
  1.9 5.5 %reshape.6.day = bf16[580,2305]{1,0:T(8,128)(2,1)} reshape(bf16[145,4,2305]{2,1,0:T(4,128)(2,1)} %bitcast.6) | data formatting | bytes 5347600 | tf_op jit(solution)/shard_map/reshape | solution.py:321
  7.3 90.7 %shard_map.64 = f32[1,256,512]{2,1,0:T(8,128)} custom-call(bf16[32,2305]{1,0:T(8,128)(2,1)} %bitcast.8, bf16[580,2305]{1,0:T(8,128)(2,1)} %reshape.6.day, bf16[580,145]{1,0:T(8,128)(2,1)} %reshape.7.bsdf, bf16[36,145,8,256]{3,2,1,0:T(8,128)(2,1)} %bitcast.5, s32[8,36]{1,0:T(8,128)} %vis_s.1, s32[8,36]{1,0:T(8,128)} %vis_s.1, s32[1,8]{1,0:T(1,128)} %bitcast.9), custom_call_target="tpu_custom_call" | custom-call | tf_op jit(solution)/shard_map/pallas_call | solution.py:330
  98.1 1.9 %copy.8 = f32[1,256,512]{2,1,0:T(8,128)} copy(f32[1,256,512]{2,1,0:T(8,128)} %shard_map.64) | data formatting | bytes 1048576

commit v2 on v1

v2 whole, which is shorter than its diff:
```python
import functools

import jax
import jax.numpy as jnp
from jax import lax
from jax.experimental import pallas as pl
from jax.experimental.pallas import tpu as pltpu
from jax.sharding import PartitionSpec as P

MESH = pl.DeviceIdType.MESH
BF = jnp.bfloat16
F32 = jnp.float32
I32 = jnp.int32

CHUNKS = 4
HC = 128
BUFS = 4


def iota(shape, dim):
    return lax.broadcasted_iota(I32, shape, dim)


def nt(a, b):
    return lax.dot_general(a, b, (((1,), (1,)), ((), ())), preferred_element_type=F32)


def mm(a, b):
    return jnp.dot(a, b, preferred_element_type=F32)


def kernel(sky, day, bsdf, view, vis_v, cnt, out,
           skyv, rawd, rawb, dayv, bsdfv, bexp, vbuf, v2,
           e0, e1, e2, e3, m0, m1, m2, m3,
           s2m, s2r, r2r, trem, selb, selp, qsel, qrest, ent, eidx, rss, rsr, own, perm,
           lsem, vsem, k1s, k1r, k2s, k2r, kcs, kcr, ls_s, ls_r,
           p1s, p1r, p2ms, p2mr, p2rs, p2rr, rs_s, rs_r):
    e1buf = [e0, e1, e2, e3]
    r2m = [m0, m1, m2, m3]
    f = lax.axis_index("facade")
    s = lax.axis_index("sensor")
    z, o = f // 2, f % 2
    x, y = s // 4, s % 4
    a = x * (1 - o) + y * o
    b = y * (1 - o) + x * o

    def sid(i, j):
        i, j = i % 4, j % 4
        return (i * 4 + j) * (1 - o) + (j * 4 + i) * o

    def first(d):
        return (f, sid(a + d, b))

    def second(d):
        return (f, sid(a, b + d))

    partner = (z * 2 + (1 - o), s)
    sends = []

    def push(src, dst, ss, rs, dev):
        cp = pltpu.make_async_remote_copy(src_ref=src, dst_ref=dst, send_sem=ss, recv_sem=rs,
                                          device_id=dev, device_id_type=MESH)
        cp.start()
        sends.append(cp)

    def arrived(dst, ss, rs, dev):
        pltpu.make_async_remote_copy(src_ref=dst, dst_ref=dst, send_sem=ss, recv_sem=rs,
                                     device_id=dev, device_id_type=MESH).wait_recv()

    def piece(i, j):
        i, j = i % 4, j % 4
        return skyv.at[o, (i + j) % 4, j * (1 - o) + i * o]

    c_sky = pltpu.make_async_copy(sky.at[pl.ds(pl.multiple_of(16 * o, 16), 16)], piece(a, b), lsem.at[0])
    c_sky.start()
    c_bs = pltpu.make_async_copy(bsdf, rawb, lsem.at[2])
    c_bs.start()
    c_day = pltpu.make_async_copy(day, rawd, lsem.at[1])
    c_day.start()

    def view_copy(j, slot):
        return pltpu.make_async_copy(view.at[j], vbuf.at[slot, pl.ds(0, 145)], vsem.at[slot])

    for q in range(BUFS):
        vbuf[q, 145:160] = jnp.zeros((15, 8, 256), BF)
        view_copy(q, q).start()

    barrier = pltpu.get_barrier_semaphore()
    for d in (1, 2, 3):
        pl.semaphore_signal(barrier, inc=1, device_id=first(d), device_id_type=MESH)
        pl.semaphore_signal(barrier, inc=1, device_id=second(d), device_id_type=MESH)
    for d in range(1, 8):
        pl.semaphore_signal(barrier, inc=1, device_id=((f + d) % 8, s), device_id_type=MESH)
    pl.semaphore_wait(barrier, 13)

    c_sky.wait()
    for d in (2, 1, 3):
        r = piece(a, b)
        push(r, r, k1s.at[d], k1r.at[d], first(d))

    vis = vis_v[...]
    slot_no = iota((8, 36), 1)
    row_no = iota((8, 36), 0)
    lim = jnp.zeros((8, 36), I32)
    for q in range(8):
        lim = jnp.where(row_no == q, cnt[0, q], lim)
    used = slot_no < lim
    src = vis >> 2
    grp = vis & 3
    later = jnp.zeros((8, 36), I32)
    for q in range(16):
        hit = used & (src == q)
        lo = jnp.min(jnp.where(hit, grp, 3))
        hi = jnp.max(jnp.where(hit, grp, 0))
        selb[2 * q:2 * q + 1, :] = jnp.full((1, 128), lo, I32)
        selb[2 * q + 1:2 * q + 2, :] = jnp.full((1, 128), hi, I32)
        later = jnp.where(hit & (grp == hi), 1, later)
    for d in (1, 2, 3):
        push(selb, selp.at[4 - d], ls_s.at[d], ls_r.at[4 - d], second(d))
    sx, sy = src >> 2, src & 3
    ia = sx * (1 - o) + sy * o
    fb = sy * (1 - o) + sx * o
    ent[...] = jnp.zeros((8, 128), I32)
    ent[:, 0:36] = jnp.where(used, fb * 8 + ia * 2 + later, 32)
    c_ent = pltpu.make_async_copy(ent, eidx, lsem.at[0])
    c_ent.start()

    c_day.wait()
    for t in range(9):
        dayv[64 * t:64 * t + 64, :] = rawd[16 * t:16 * t + 16].reshape(64, 2305)
    dayv[576:580, :] = rawd[144]

    for d in (1, 3, 2):
        arrived(piece(a - d, b), k1s.at[d], k1r.at[d], first(d))
    for c in range(CHUNKS):
        for d in (2, 1, 3):
            r = piece(c - b + 4, b)
            push(r, r, k2s.at[d, c], k2r.at[d, c], second(d))

    c_bs.wait()
    for t in range(9):
        bsdfv[64 * t:64 * t + 64, :] = rawb[16 * t:16 * t + 16].reshape(64, 145)
    bsdfv[576:580, :] = rawb[144]
    w1 = (iota((580, 145), 0) // 4 == iota((580, 145), 1)).astype(F32).astype(BF)
    c1 = nt(w1, bsdfv[...]).astype(BF)
    pr, pc = iota((580, 640), 0), iota((580, 640), 1)
    pk, pg = pr // 4, pr % 4
    hit = (pc < 512) & (pc == pg * 128 + pk) & (pk < 128)
    hit = hit | ((pk >= 128) & (pc - 512 == 17 * pg + pk - 128))
    c2 = mm(c1, hit.astype(F32).astype(BF))
    rr = pc - 512
    gcol = jnp.where(pc < 512, pc // 128,
                     (rr >= 17).astype(I32) + (rr >= 34).astype(I32) + (rr >= 51).astype(I32))
    bexp[...] = jnp.where(pg == gcol, c2, 0.0).astype(BF)

    ur, uc = iota((256, 256), 0), iota((256, 256), 1)
    perm[...] = ((uc % 8 == ur // 32) & (uc // 8 == ur % 32)).astype(F32).astype(BF)

    def permute(lo, hi):
        def body(j, carry):
            slot = j % BUFS
            view_copy(j, slot).wait()
            for t in range(5):
                xin = vbuf[slot, 32 * t:32 * t + 32].reshape(256, 256)
                res = mm(perm[...], xin).astype(BF)
                v2[j, :, 32 * t:32 * t + 32, :] = res.reshape(8, 32, 256)

            @pl.when(j + BUFS < 36)
            def _():
                view_copy(j + BUFS, slot).start()
            return carry
        lax.fori_loop(lo, hi, body, 0)

    def gather(c):
        for d in (1, 3, 2):
            arrived(piece(c - b + d + 4, b - d), k2s.at[d, c], k2r.at[d, c], second(d))
        r = skyv.at[o, c]
        push(r, r, kcs.at[c], kcr.at[c], partner)

    def daylit(c):
        arrived(skyv.at[1 - o, c], kcs.at[c], kcr.at[c], partner)
        lhs = jnp.concatenate([skyv[h, c, q] for q in range(4) for h in range(2)], axis=0)
        dt = nt(lhs, dayv[...]).astype(BF)
        e = mm(dt, bexp[...]).astype(BF)
        for q in range(5):
            e1buf[c][a, q] = e[:, 128 * q:128 * q + 128]
        r = e1buf[c].at[a]
        for d in (2, 1, 3):
            push(r, r, p1s.at[c, d], p1r.at[c, d], first(d))

    def make_q(d):
        lane, col = iota((128, 128), 0), iota((128, 128), 1)
        for i in range(4):
            acc = jnp.zeros((128, 128), F32)
            for m in range(2):
                n = 2 * i + m
                if n < 7:
                    sel = selp[d, pl.ds(sid(i, b) * 2 + m, 1), :]
                    hit = (lane - col == 17 * sel - 17 * n) & (col >= 17 * n) & (col < 17 * n + 17)
                    acc = acc + hit.astype(F32)
            qsel[d, 128 * i:128 * i + 128, :] = acc.astype(BF)
        row, lan = iota((32, 128), 0), iota((32, 128), 1)
        sel = selp[d, pl.ds(sid(3, b) * 2 + 1, 1), :]
        qrest[d] = ((lan - row == 17 * sel) & (row < 17)).astype(F32).astype(BF)

    def select(c):
        for d in (1, 3, 2):
            arrived(e1buf[c].at[(a - d) % 4], p1s.at[c, d], p1r.at[c, d], first(d))
        lhs = jnp.concatenate([e1buf[c][i, 4] for i in range(4)], axis=1)
        for d in (2, 1, 3, 0):
            for i in range(4):
                planes = [e1buf[c][i, g].astype(F32) for g in range(4)]
                for m in range(2):
                    sel = selp[d, pl.ds(sid(i, b) * 2 + m, 1), :]
                    pick = planes[0]
                    for g in range(1, 4):
                        pick = jnp.where(sel == g, planes[g], pick)
                    pick = pick.astype(BF)
                    if d:
                        s2m[c, d - 1, 2 * i + m] = pick
                    else:
                        r2m[c][b * 8 + 2 * i + m] = pick
            if d:
                push(s2m.at[c, d - 1], r2m[c].at[pl.ds(b * 8, 8)], p2ms.at[c, d], p2mr.at[c, d], second(d))
            rem = mm(lhs, qsel[d]).astype(BF)
            rest = nt(qrest[d], e1buf[c][3, 4]).astype(BF)
            if d:
                s2r[c, d - 1, 0:128] = rem
                s2r[c, d - 1, 128:160] = rest
                push(s2r.at[c, d - 1], r2r.at[c, b], p2rs.at[c, d], p2rr.at[c, d], second(d))
            else:
                r2r[c, b, 0:128] = rem
                r2r[c, b, 128:160] = rest

    def received(c):
        for d in (1, 3, 2):
            j = (b - d) % 4
            arrived(r2m[c].at[pl.ds(j * 8, 8)], p2ms.at[c, d], p2mr.at[c, d], second(d))
            arrived(r2r.at[c, j], p2rs.at[c, d], p2rr.at[c, d], second(d))
        keep = iota((HC, 128), 1) < 17
        eye = (iota((HC, HC), 0) == iota((HC, HC), 1)).astype(F32).astype(BF)

        def body(fb, carry):
            plane = r2r[c, fb, 0:128].astype(F32)
            for n in range(7):
                v = plane if n == 0 else pltpu.roll(plane, 128 - 17 * n, 1)
                trem[fb * 8 + n] = jnp.where(keep, v, 0.0)[:, :32].astype(BF)
            trem[fb * 8 + 7] = nt(eye, r2r[c, fb, 128:160]).astype(BF)
            return carry
        lax.fori_loop(0, 4, body, 0)

    def compute(c):
        def block(i):
            bb = (f + 1 + i) % 8
            acc = None
            for j in range(36):
                e = eidx[bb, j]
                lhs = jnp.concatenate([r2m[c][e], trem[e]], axis=1)
                p = mm(lhs, v2[j, bb])
                acc = p if acc is None else acc + p
            return acc

        def body(i, carry):
            rss[c, i] = block(i).astype(BF)
            pltpu.make_async_remote_copy(
                src_ref=rss.at[c, i], dst_ref=rsr.at[c, i], send_sem=rs_s.at[c], recv_sem=rs_r.at[c],
                device_id=((f + 1 + i) % 8, s), device_id_type=MESH).start()
            return carry
        lax.fori_loop(0, 7, body, 0)
        own[c] = block(7)

    def rs_all(c):
        return pltpu.make_async_remote_copy(
            src_ref=rss.at[c], dst_ref=rsr.at[c], send_sem=rs_s.at[c], recv_sem=rs_r.at[c],
            device_id=((f + 1) % 8, s), device_id_type=MESH)

    def reduce(c):
        rs_all(c).wait_recv()
        acc = own[c]
        for i in range(7):
            acc = acc + rsr[c, i].astype(F32)
        t = acc.T
        for q in range(4):
            lo = 128 * ((c - q) % 4) + 32 * q
            out[0, :, lo:lo + 32] = t[:, 32 * q:32 * q + 32]

    for c in range(CHUNKS):
        r2m[c][32] = jnp.zeros((HC, 128), BF)
    trem[32] = jnp.zeros((HC, 32), BF)
    permute(0, 10)
    gather(0)
    gather(1)
    daylit(0)
    gather(2)
    daylit(1)
    gather(3)
    selp[0] = selb[...]
    for d in (1, 2, 3):
        arrived(selp.at[d], ls_s.at[d], ls_r.at[d], second(d))
    for d in range(4):
        make_q(d)
    permute(10, 14)
    select(0)
    daylit(2)
    permute(14, 20)
    select(1)
    daylit(3)
    permute(20, 28)
    select(2)
    permute(28, 36)
    c_ent.wait()
    received(0)
    compute(0)
    select(3)
    for c in range(1, CHUNKS):
        received(c)
        compute(c)
        reduce(c - 1)
    reduce(CHUNKS - 1)
    for cp in sends:
        cp.wait_send()
    for c in range(CHUNKS):
        rs_all(c).wait_send()


def on_device(sky, daylight, bsdf, view, visible, counts):
    V = pltpu.VMEM
    D = pltpu.SemaphoreType.DMA
    anyspec = pl.BlockSpec(memory_space=pl.ANY)
    vm = pl.BlockSpec(memory_space=pltpu.VMEM)
    sm = pl.BlockSpec(memory_space=pltpu.SMEM)
    return pl.pallas_call(
        kernel,
        out_shape=jax.ShapeDtypeStruct((1, 256, 512), F32),
        in_specs=[anyspec, anyspec, anyspec, anyspec, vm, sm],
        out_specs=vm,
        scratch_shapes=[
            V((2, 4, 4, 16, 2305), BF), V((145, 4, 2305), BF), V((145, 4, 145), BF),
            V((580, 2305), BF), V((580, 145), BF), V((580, 640), BF),
            V((BUFS, 160, 8, 256), BF), V((36, 8, 160, 256), BF),
            *[V((4, 5, HC, 128), BF)] * 4, *[V((33, HC, 128), BF)] * 4,
            V((CHUNKS, 3, 8, HC, 128), BF), V((CHUNKS, 3, 160, 128), BF),
            V((CHUNKS, 4, 160, 128), BF), V((33, HC, 32), BF),
            V((32, 128), I32), V((4, 32, 128), I32), V((4, 512, 128), BF), V((4, 32, 128), BF),
            V((8, 128), I32), pltpu.SMEM((8, 128), I32),
            V((CHUNKS, 7, HC, 256), BF), V((CHUNKS, 7, HC, 256), BF), V((CHUNKS, HC, 256), F32),
            V((256, 256), BF),
            D((3,)), D((BUFS,)), D((4,)), D((4,)), D((4, 4)), D((4, 4)), D((4,)), D((4,)),
            D((4,)), D((4,)),
            *[D((CHUNKS, 4))] * 6, D((CHUNKS,)), D((CHUNKS,)),
        ],
        compiler_params=pltpu.CompilerParams(
            collective_id=0, has_side_effects=True, vmem_limit_bytes=60 * 2**20),
    )(sky.T, daylight.transpose(1, 0, 2), bsdf.transpose(1, 0, 2), view.transpose(1, 2, 0, 3),
      visible, counts.T)


def solution(mesh):
    placed = (
        P(None, "sensor"),
        P(("facade", "sensor"), None, None),
        P(("facade", "sensor"), None, None),
        P("sensor", "facade", None, None),
        P("sensor", "facade"),
        P("sensor", "facade"),
    )
    return jax.shard_map(
        on_device,
        mesh=mesh,
        in_specs=placed,
        out_specs=P(("sensor", "facade"), None, None),
        check_vma=False,
    )
```

time: 100 us -> 83.1 us (0.83)
  Pallas kernels: 90.7 us -> 81.1 us
  local copies, waits for them, and re-layouts: 9.2 us -> 1.87 us
    pallas_call x1, Pallas kernels: 90.7 us -> 81.1 us  [on_device(): pl.pallas_call(kernel, out_shape=jax.ShapeDtypeStruct((1, 256, 512), F32)...]
    reshape x2 -> x0, local copies, waits for them, and re-layouts: 7.33 us -> none  [the longest x1 5.47 us: on_device(): day = daylight.transpose(1, 0, 2).reshape(580, 2305)]
where the time goes in v2:
time: 83.1 us; the launch traced here: 82.9 us
  Pallas kernels  81.1 us (98%)
  local copies, waits for them, and re-layouts  1.87 us (2%)
    pallas_call x1, Pallas kernels, on_device(): pl.pallas_call(kernel, out_shape=jax.ShapeDtypeStruct((1, 256, 512), F32)...  81.1 us
    unnamed x1, local copies, waits for them, and re-layouts  1.87 us

profile of v2, /device:TPU:1, one launch (start us, length us, event | category | flops | bytes accessed | tf_op | source)
XLA Modules:
  0.0 82.9 jit_solution(16122953731148201103)
XLA Ops:
  0.0 81.1 %shard_map.64 = f32[1,256,512]{2,1,0:T(8,128)} custom-call(bf16[32,2305]{1,0:T(8,128)(2,1)} %bitcast.8, bf16[145,4,2305]{2,1,0:T(4,128)(2,1)} %bitcast.6, bf16[145,4,145]{2,1,0:T(4,128)(2,1)} %bitcast.7, bf16[36,145,8,256]{3,2,1,0:T(8,128)(2,1)} %bitcast.5, s32[8,36]{1,0:T(8,128)} %vis_v.1, s32[1,8]{1,0:T(1,128)} %bitcast.9), custom_call_target="tpu_custom_call" | custom-call | tf_op jit(solution)/shard_map/pallas_call | solution.py:332
  81.1 1.9 %copy.8 = f32[1,256,512]{2,1,0:T(8,128)} copy(f32[1,256,512]{2,1,0:T(8,128)} %shard_map.64) | data formatting | bytes 1048576

commit v3 on v2

--- a/solution.py
+++ b/solution.py
@@ -30,9 +30,9 @@
 
 
 def kernel(sky, day, bsdf, view, vis_v, cnt, out,
-           skyv, rawd, rawb, dayv, bsdfv, bexp, vbuf, v2,
+           skyv, rawd, rawb, dayv, bsdfv, bexp, vbuf, v2m, v2r,
            e0, e1, e2, e3, m0, m1, m2, m3,
-           s2m, s2r, r2r, trem, selb, selp, qsel, qrest, ent, eidx, rss, rsr, own, perm,
+           s2m, s2r, r2r, trem, selb, selp, qsel, qrest, place, ent, eidx, rss, rsr, own, perm,
            lsem, vsem, k1s, k1r, k2s, k2r, kcs, kcr, ls_s, ls_r,
            p1s, p1r, p2ms, p2mr, p2rs, p2rr, rs_s, rs_r):
     e1buf = [e0, e1, e2, e3]
@@ -125,17 +125,17 @@
     c_ent = pltpu.make_async_copy(ent, eidx, lsem.at[0])
     c_ent.start()
 
-    c_day.wait()
-    for t in range(9):
-        dayv[64 * t:64 * t + 64, :] = rawd[16 * t:16 * t + 16].reshape(64, 2305)
-    dayv[576:580, :] = rawd[144]
-
     for d in (1, 3, 2):
         arrived(piece(a - d, b), k1s.at[d], k1r.at[d], first(d))
     for c in range(CHUNKS):
         for d in (2, 1, 3):
             r = piece(c - b + 4, b)
             push(r, r, k2s.at[d, c], k2r.at[d, c], second(d))
+
+    c_day.wait()
+    for t in range(9):
+        dayv[64 * t:64 * t + 64, :] = rawd[16 * t:16 * t + 16].reshape(64, 2305)
+    dayv[576:580, :] = rawd[144]
 
     c_bs.wait()
     for t in range(9):
@@ -163,7 +163,11 @@
             for t in range(5):
                 xin = vbuf[slot, 32 * t:32 * t + 32].reshape(256, 256)
                 res = mm(perm[...], xin).astype(BF)
-                v2[j, :, 32 * t:32 * t + 32, :] = res.reshape(8, 32, 256)
+                res = res.reshape(8, 32, 256)
+                if t < 4:
+                    v2m[j // 2, :, pl.ds(pl.multiple_of(128 * (j % 2) + 32 * t, 32), 32), :] = res
+                else:
+                    v2r[j // 8, :, pl.ds(pl.multiple_of(32 * (j % 8), 32), 32), :] = res
 
             @pl.when(j + BUFS < 36)
             def _():
@@ -185,8 +189,17 @@
         for q in range(5):
             e1buf[c][a, q] = e[:, 128 * q:128 * q + 128]
         r = e1buf[c].at[a]
-        for d in (2, 1, 3):
+        for d in (1, 3):
             push(r, r, p1s.at[c, d], p1r.at[c, d], first(d))
+
+    def across(c, d, at):
+        return e1buf[c].at[at % 4, :, pl.ds(0 if d == 1 else HC // 2, HC // 2)]
+
+    def forward(c):
+        for d in (1, 3):
+            arrived(e1buf[c].at[(a - d) % 4], p1s.at[c, d], p1r.at[c, d], first(d))
+            r = across(c, d, a - d + 4)
+            push(r, r, p1s.at[c, d - 1], p1r.at[c, d - 1], first(d))
 
     def make_q(d):
         lane, col = iota((128, 128), 0), iota((128, 128), 1)
@@ -204,8 +217,8 @@
         qrest[d] = ((lan - row == 17 * sel) & (row < 17)).astype(F32).astype(BF)
 
     def select(c):
-        for d in (1, 3, 2):
-            arrived(e1buf[c].at[(a - d) % 4], p1s.at[c, d], p1r.at[c, d], first(d))
+        for d in (1, 3):
+            arrived(across(c, d, a + 2), p1s.at[c, d - 1], p1r.at[c, d - 1], first(d))
         lhs = jnp.concatenate([e1buf[c][i, 4] for i in range(4)], axis=1)
         for d in (2, 1, 3, 0):
             for i in range(4):
@@ -237,34 +250,46 @@
             j = (b - d) % 4
             arrived(r2m[c].at[pl.ds(j * 8, 8)], p2ms.at[c, d], p2mr.at[c, d], second(d))
             arrived(r2r.at[c, j], p2rs.at[c, d], p2rr.at[c, d], second(d))
-        keep = iota((HC, 128), 1) < 17
         eye = (iota((HC, HC), 0) == iota((HC, HC), 1)).astype(F32).astype(BF)
+        wide = (iota((32, 128), 0) == iota((32, 128), 1) % 32).astype(F32).astype(BF)
 
         def body(fb, carry):
-            plane = r2r[c, fb, 0:128].astype(F32)
+            plane = r2r[c, fb, 0:128]
             for n in range(7):
-                v = plane if n == 0 else pltpu.roll(plane, 128 - 17 * n, 1)
-                trem[fb * 8 + n] = jnp.where(keep, v, 0.0)[:, :32].astype(BF)
-            trem[fb * 8 + 7] = nt(eye, r2r[c, fb, 128:160]).astype(BF)
+                trem[fb * 8 + n] = mm(plane, place[n]).astype(BF)
+            last = nt(eye, r2r[c, fb, 128:160]).astype(BF)
+            trem[fb * 8 + 7] = mm(last, wide).astype(BF)
             return carry
         lax.fori_loop(0, 4, body, 0)
 
+    def dest(i):
+        return ((z + 1 + i // 2) % 4) * 2 + (o + 1 + i % 2) % 2
+
     def compute(c):
         def block(i):
-            bb = (f + 1 + i) % 8
+            bb = dest(i)
             acc = None
-            for j in range(36):
-                e = eidx[bb, j]
-                lhs = jnp.concatenate([r2m[c][e], trem[e]], axis=1)
-                p = mm(lhs, v2[j, bb])
+            es = [eidx[bb, j] for j in range(36)]
+            for j in range(18):
+                lhs = jnp.concatenate([r2m[c][es[2 * j]], r2m[c][es[2 * j + 1]]], axis=1)
+                p = mm(lhs, v2m[j, bb])
                 acc = p if acc is None else acc + p
-            return acc
+            quarter = iota((HC, 128), 1) // 32
+            for q in range(9):
+                h = trem[es[4 * q]]
+                for k in range(1, 4):
+                    h = jnp.where(quarter == k, trem[es[4 * q + k]], h)
+                if q % 2 == 0:
+                    prev = h
+                else:
+                    acc = acc + mm(jnp.concatenate([prev, h], axis=1), v2r[q // 2, bb])
+            return acc + mm(prev, v2r[4, bb, 0:128])
 
         def body(i, carry):
             rss[c, i] = block(i).astype(BF)
             pltpu.make_async_remote_copy(
                 src_ref=rss.at[c, i], dst_ref=rsr.at[c, i], send_sem=rs_s.at[c], recv_sem=rs_r.at[c],
-                device_id=((f + 1 + i) % 8, s), device_id_type=MESH).start()
+                device_id=(dest(i), s), device_id_type=MESH).start()
             return carry
         lax.fori_loop(0, 7, body, 0)
         own[c] = block(7)
@@ -272,7 +297,7 @@
     def rs_all(c):
         return pltpu.make_async_remote_copy(
             src_ref=rss.at[c], dst_ref=rsr.at[c], send_sem=rs_s.at[c], recv_sem=rs_r.at[c],
-            device_id=((f + 1) % 8, s), device_id_type=MESH)
+            device_id=(dest(0), s), device_id_type=MESH)
 
     def reduce(c):
         rs_all(c).wait_recv()
@@ -286,26 +311,34 @@
 
     for c in range(CHUNKS):
         r2m[c][32] = jnp.zeros((HC, 128), BF)
-    trem[32] = jnp.zeros((HC, 32), BF)
-    permute(0, 10)
+    trem[32] = jnp.zeros((HC, 128), BF)
+    for n in range(7):
+        place[n] = (iota((128, 128), 0) == iota((128, 128), 1) % 32 + 17 * n).astype(F32).astype(BF) * (
+            iota((128, 128), 1) % 32 < 17).astype(F32).astype(BF)
+    permute(0, 8)
     gather(0)
     gather(1)
     daylit(0)
     gather(2)
     daylit(1)
     gather(3)
+    daylit(2)
+    daylit(3)
     selp[0] = selb[...]
     for d in (1, 2, 3):
         arrived(selp.at[d], ls_s.at[d], ls_r.at[d], second(d))
     for d in range(4):
         make_q(d)
-    permute(10, 14)
+    permute(8, 12)
+    forward(0)
+    forward(1)
+    permute(12, 18)
+    forward(2)
     select(0)
-    daylit(2)
-    permute(14, 20)
+    forward(3)
+    permute(18, 22)
     select(1)
-    daylit(3)
-    permute(20, 28)
+    permute(22, 28)
     select(2)
     permute(28, 36)
     c_ent.wait()
@@ -337,11 +370,11 @@
         scratch_shapes=[
             V((2, 4, 4, 16, 2305), BF), V((145, 4, 2305), BF), V((145, 4, 145), BF),
             V((580, 2305), BF), V((580, 145), BF), V((580, 640), BF),
-            V((BUFS, 160, 8, 256), BF), V((36, 8, 160, 256), BF),
+            V((BUFS, 160, 8, 256), BF), V((18, 8, 256, 256), BF), V((5, 8, 256, 256), BF),
             *[V((4, 5, HC, 128), BF)] * 4, *[V((33, HC, 128), BF)] * 4,
             V((CHUNKS, 3, 8, HC, 128), BF), V((CHUNKS, 3, 160, 128), BF),
-            V((CHUNKS, 4, 160, 128), BF), V((33, HC, 32), BF),
-            V((32, 128), I32), V((4, 32, 128), I32), V((4, 512, 128), BF), V((4, 32, 128), BF),
+            V((CHUNKS, 4, 160, 128), BF), V((33, HC, 128), BF),
+            V((32, 128), I32), V((4, 32, 128), I32), V((4, 512, 128), BF), V((4, 32, 128), BF), V((7, 128, 128), BF),
             V((8, 128), I32), pltpu.SMEM((8, 128), I32),
             V((CHUNKS, 7, HC, 256), BF), V((CHUNKS, 7, HC, 256), BF), V((CHUNKS, HC, 256), F32),
             V((256, 256), BF),

time: 83.1 us -> 78.1 us (0.940)
  Pallas kernels: 81.1 us -> 75.5 us
    pallas_call x1, Pallas kernels: 81.1 us -> 75.5 us  [on_device(): pl.pallas_call(kernel, out_shape=jax.ShapeDtypeStruct((1, 256, 512), F32)...]
where the time goes in v3:
time: 78.1 us; the launch traced here: 77.4 us
  Pallas kernels  75.5 us (97%)
  local copies, waits for them, and re-layouts  1.87 us (2%)
    pallas_call x1, Pallas kernels, on_device(): pl.pallas_call(kernel, out_shape=jax.ShapeDtypeStruct((1, 256, 512), F32)...  75.5 us
    unnamed x1, local copies, waits for them, and re-layouts  1.87 us

profile of v3, /device:TPU:1, one launch (start us, length us, event | category | flops | bytes accessed | tf_op | source)
XLA Modules:
  0.0 77.4 jit_solution(8284063727855295878)
XLA Ops:
  0.0 75.5 %shard_map.64 = f32[1,256,512]{2,1,0:T(8,128)} custom-call(bf16[32,2305]{1,0:T(8,128)(2,1)} %bitcast.8, bf16[145,4,2305]{2,1,0:T(4,128)(2,1)} %bitcast.6, bf16[145,4,145]{2,1,0:T(4,128)(2,1)} %bitcast.7, bf16[36,145,8,256]{3,2,1,0:T(8,128)(2,1)} %bitcast.5, s32[8,36]{1,0:T(8,128)} %vis_v.1, s32[1,8]{1,0:T(1,128)} %bitcast.9), custom_call_target="tpu_custom_call" | custom-call | tf_op jit(solution)/shard_map/pallas_call | solution.py:365
  75.5 1.9 %copy.8 = f32[1,256,512]{2,1,0:T(8,128)} copy(f32[1,256,512]{2,1,0:T(8,128)} %shard_map.64) | data formatting | bytes 1048576

commit v4 on v3

--- a/solution.py
+++ b/solution.py
@@ -260,7 +260,8 @@
             last = nt(eye, r2r[c, fb, 128:160]).astype(BF)
             trem[fb * 8 + 7] = mm(last, wide).astype(BF)
             return carry
-        lax.fori_loop(0, 4, body, 0)
+        for fb in range(4):
+            body(fb, 0)
 
     def dest(i):
         return ((z + 1 + i // 2) % 4) * 2 + (o + 1 + i % 2) % 2
@@ -285,14 +286,24 @@
                     acc = acc + mm(jnp.concatenate([prev, h], axis=1), v2r[q // 2, bb])
             return acc + mm(prev, v2r[4, bb, 0:128])
 
-        def body(i, carry):
-            rss[c, i] = block(i).astype(BF)
-            pltpu.make_async_remote_copy(
-                src_ref=rss.at[c, i], dst_ref=rsr.at[c, i], send_sem=rs_s.at[c], recv_sem=rs_r.at[c],
-                device_id=(dest(i), s), device_id_type=MESH).start()
+        def body(k, carry):
+            i = 2 * k
+            even, odd = block(i), block(i + 1)
+            rss[c, i] = even.astype(BF)
+            rs_copy(c, i).start()
+            own[c] = odd
+
+            @pl.when(k < 3)
+            def _():
+                rss[c, i + 1] = odd.astype(BF)
+                rs_copy(c, i + 1).start()
             return carry
-        lax.fori_loop(0, 7, body, 0)
-        own[c] = block(7)
+        lax.fori_loop(0, 4, body, 0)
+
+    def rs_copy(c, i):
+        return pltpu.make_async_remote_copy(
+            src_ref=rss.at[c, i], dst_ref=rsr.at[c, i], send_sem=rs_s.at[c], recv_sem=rs_r.at[c],
+            device_id=(dest(i), s), device_id_type=MESH)
 
     def rs_all(c):
         return pltpu.make_async_remote_copy(

time: 78.1 us -> 77.2 us (0.988)
  no operation moved by 1% of the time
where the time goes in v4:
time: 77.2 us; the launch traced here: 77 us
  Pallas kernels  75.1 us (97%)
  local copies, waits for them, and re-layouts  1.87 us (2%)
    pallas_call x1, Pallas kernels, on_device(): pl.pallas_call(kernel, out_shape=jax.ShapeDtypeStruct((1, 256, 512), F32)...  75.1 us
    unnamed x1, local copies, waits for them, and re-layouts  1.87 us

profile of v4, /device:TPU:1, one launch (start us, length us, event | category | flops | bytes accessed | tf_op | source)
XLA Modules:
  0.0 77.0 jit_solution(16107318309477598785)
XLA Ops:
  0.0 75.1 %shard_map.64 = f32[1,256,512]{2,1,0:T(8,128)} custom-call(bf16[32,2305]{1,0:T(8,128)(2,1)} %bitcast.8, bf16[145,4,2305]{2,1,0:T(4,128)(2,1)} %bitcast.6, bf16[145,4,145]{2,1,0:T(4,128)(2,1)} %bitcast.7, bf16[36,145,8,256]{3,2,1,0:T(8,128)(2,1)} %bitcast.5, s32[8,36]{1,0:T(8,128)} %vis_v.1, s32[1,8]{1,0:T(1,128)} %bitcast.9), custom_call_target="tpu_custom_call" | custom-call | tf_op jit(solution)/shard_map/pallas_call | solution.py:376
  75.2 1.9 %copy.8 = f32[1,256,512]{2,1,0:T(8,128)} copy(f32[1,256,512]{2,1,0:T(8,128)} %shard_map.64) | data formatting | bytes 1048576
